TPU v7x, 32 devices: a whole 2x2x4 slice. The times are simulated.
32 devices in a mesh: ctx: 8 (over z, core), tp: 4 (over y, x).
Axes of the slice: x: 2, y: 2, z: 4, core: 2. Of those that a mesh axis runs over, the one named last changes fastest.
Arguments:
- features: bfloat16 [1024, 3, 8192], P('ctx', None, 'tp'), may hold values from -6 to 6
- short_filter: float32 [3, 3, 8192], P(None, None, 'tp'), may hold values from -3 to 3
- decay_rate: float32 [16, 8192], P(None, 'tp'), may hold values from 2e-05 to 0.04
- residue: float32 [16, 8192], P(None, 'tp'), may hold values from -2 to 2
- skip: float32 [8192], P('tp'), may hold values from -2 to 2
- out_weight: bfloat16 [8192, 8192], P('tp', 'ctx'), may hold values from -0.09375 to 0.09375
Outputs:
- mixed: bfloat16 [1024, 8192], P('ctx', 'tp')
All inputs are finite; a program needn't handle non-finite values.
Results may differ from a plain program's by a relative error of at most 0.0049.
Values may be sent and summed in bfloat16 or wider, within the bound.
A program may use at most 128 MiB of HBM per device.

v0:
```python
import jax
import jax.numpy as jnp
from jax import lax
from jax.sharding import PartitionSpec as P

BLOCK = 32


def from_behind(value, axis, by):
    size = lax.axis_size(axis)
    pairs = [(i, i + by) for i in range(size) if 0 <= i + by < size]
    return lax.ppermute(value, axis, pairs)


def carried_in(value, axis, combine, identity):
    size, index = (lax.axis_size(axis), lax.axis_index(axis))
    everything = jax.tree.map(lambda part: lax.all_gather(part, axis), value)
    start = jax.tree.map(
        lambda part, zero: jnp.broadcast_to(jnp.asarray(zero, part.dtype), part.shape),
        value,
        identity,
    )

    def step(k, before):
        reached = k < index
        new = combine(before, jax.tree.map(lambda part: part[k], everything))
        return jax.tree.map(lambda a, b: jnp.where(reached, a, b), new, before)

    return lax.fori_loop(0, size, step, start)


def shards(features, short_filter, decay_rate, residue, skip, out_weight):
    positions = features.shape[0]
    tap_count = short_filter.shape[0]
    channels = features.shape[2]
    halo_rows = from_behind(features[positions - (tap_count - 1) :], "ctx", 1)
    extended = jnp.concatenate([halo_rows, features], axis=0).astype(jnp.float32)
    filtered = jnp.zeros((positions, 3, channels), jnp.float32)
    for tap_index in range(tap_count):
        begin = tap_count - 1 - tap_index
        filtered = filtered + short_filter[tap_index][None] * extended[begin : begin + positions]
    query = filtered[:, 0]
    drive = filtered[:, 1] * filtered[:, 2]
    gain = residue * jnp.sqrt(-jnp.expm1(-2.0 * decay_rate))
    block_len = BLOCK
    block_count = positions // block_len
    offsets = jnp.arange(block_len, dtype=jnp.float32)
    powers = jnp.exp(-decay_rate[None] * offsets[:, None, None])
    kernel = jnp.sum(gain[None] * powers, axis=1)
    lag_table = jnp.arange(block_len)[:, None] - jnp.arange(block_len)[None, :]
    toeplitz = jnp.where(
        (lag_table >= 0)[:, :, None], kernel[jnp.clip(lag_table, 0, block_len - 1)], 0.0
    )
    blocks = drive.reshape(block_count, block_len, channels)
    inside = jnp.einsum("tsc,nsc->ntc", toeplitz, blocks, precision=lax.Precision.HIGHEST)
    block_ends = jnp.einsum("smc,nsc->nmc", powers[::-1], blocks, precision=lax.Precision.HIGHEST)
    block_decay = jnp.exp(-decay_rate * block_len)

    def advance(state, block_end):
        return (block_decay * state + block_end, state)

    zero_state = jnp.zeros_like(decay_rate)
    local_end, starts = lax.scan(advance, zero_state, block_ends)
    device_decay = jnp.exp(-decay_rate * positions)

    def combine(earlier, later):
        return (earlier[0] * later[0], later[0] * earlier[1] + later[1])

    carried_pair = carried_in(
        (device_decay, local_end), "ctx", combine, (jnp.ones_like(decay_rate), zero_state)
    )
    incoming = carried_pair[1]
    block_offsets = jnp.arange(block_count, dtype=jnp.float32) * block_len
    leading = jnp.exp(-decay_rate[None] * block_offsets[:, None, None])
    starts = starts + leading * incoming[None]
    after_start = gain[None] * jnp.exp(-decay_rate[None] * (offsets + 1.0)[:, None, None])
    carried = jnp.einsum("tmc,nmc->ntc", after_start, starts, precision=lax.Precision.HIGHEST)
    response = (inside + carried).reshape(positions, channels) + skip[None] * drive
    gated = (query * response).astype(jnp.bfloat16)
    partial_sums = jnp.dot(
        gated,
        lax.all_gather(out_weight, "ctx", axis=1, tiled=True),
        preferred_element_type=jnp.float32,
    )
    return lax.psum_scatter(partial_sums, "tp", scatter_dimension=1, tiled=True).astype(
        jnp.bfloat16
    )


def solution(mesh):
    in_specs = (
        P("ctx", None, "tp"),
        P(None, None, "tp"),
        P(None, "tp"),
        P(None, "tp"),
        P("tp"),
        P("tp", "ctx"),
    )
    out_specs = P("ctx", "tp")
    return jax.shard_map(shards, mesh=mesh, in_specs=in_specs, out_specs=out_specs, check_vma=False)
```

profile of v0, /device:TPU:6, one launch (start us, length us, event | category | flops | bytes accessed | tf_op | source)
XLA Modules:
  0.0 490.8 jit_solution(9834063404882974230)
XLA Ops:
  6.5 0.0 all-gather.8.cloned.1.call-start
  6.5 0.9 slice.31
  7.5 1.7 collective-permute-start
  9.2 1.7 multiply_exponential_fusion.1
  10.9 0.0 all-gather.8.cloned.1.call-update
  11.0 0.0 all-gather.10.cloned.1.call-start
  11.0 0.3 copy.24
  11.3 0.2 copy-done.4
  11.6 0.3 copy.23
  11.9 0.0 copy-start.9
  11.9 13.8 %multiply_exponential_fusion = (f32[32,16,2048]{0,1,2:T(8,128)}, f32[32,2048]{0,1:T(8,128)}) fusion(f32[16,2048]{0,1:T(8,128)S(1)} %copy.24, f32[16,2048]{0,1:T(8,128)S(1)} %copy.23), kind=kLoop, calls=%fused_computation.14 | loop fusion | flops 3080192 | bytes 4718592 | tf_op jit(solution)/shard_map/exp | solution.py:48
  25.7 0.0 copy-done.1
  25.7 0.0 copy-done.9
  25.7 0.6 slice_bitcast_fusion.3
  26.4 25.1 %rev.3 = f32[32,16,2048]{0,1,2:T(8,128)} reverse(f32[32,16,2048]{0,1,2:T(8,128)} %get-tuple-element.201), dimensions={0} | reverse | bytes 8388608 | tf_op jit(solution)/shard_map/rev | solution.py:56
  51.5 0.0 collective-permute-done
  51.5 0.5 maximum_convert_fusion
  52.0 0.2 copy-done.6
  52.2 0.0 copy-done.7
  52.2 0.0 copy-done.8
  52.3 0.9 fusion.12
  53.2 1.1 slice_multiply_fusion.3
  54.3 4.6 copy.27
  58.9 30.2 %convolution_bitcast_fusion = f32[4,16,2048]{1,0,2:T(4,128)} fusion(f32[4,32,2048]{1,0,2:T(4,128)} %copy.27, f32[32,16,2048]{0,1,2:T(8,128)} %rev.3), kind=kOutput, calls=%fused_computation.25 | convolution fusion | flops 50331648 | bytes 5767168 | tf_op jit(solution)/shard_map/smc,nsc->nmc/dot_general | solution.py:56
  89.1 4.5 copy.29
  93.6 6.7 %while.27 = (s32[]{:T(128)}, f32[16,2048]{1,0:T(8,128)S(1)}, f32[4,16,2048]{2,1,0:T(8,128)}, f32[16,2048]{1,0:T(8,128)S(1)}, f32[4,16,2048]{2,1,0:T(8,128)}, /*index=5*/s32[]{:T(128)}, s32[]{:T(128)}) while((s32[]{:T(128)}, f32[16,2048]{1,0:T(8,128)S(1)}, f32[4,16,2048]{2,1,0:T(8,128)}, f32[16,2048]{1,0:T(8,128)S(1)}, ...), condition=%wide.region_2.3_spmd.clone, body=%wide.region_1.2_spmd.clone.sunk | while | flops 131075 | bytes 787036 | solution.py:63
  93.6 0.7 bitcast_dynamic-update-slice_fusion.2
  94.2 1.0 bitcast_add_fusion.3
  95.2 0.7 bitcast_dynamic-update-slice_fusion.2
  95.9 1.0 bitcast_add_fusion.3
  96.9 0.7 bitcast_dynamic-update-slice_fusion.2
  97.6 1.0 bitcast_add_fusion.3
  98.6 0.7 bitcast_dynamic-update-slice_fusion.2
  99.2 1.0 bitcast_add_fusion.3
  100.2 0.6 copy-done
  100.9 0.0 all-gather.10.cloned.1.call-update
  100.9 0.0 all-gather.6.cloned.1.call-start
  101.0 0.7 all-gather.6.cloned.1.call-update
  101.7 0.2 reduce-scatter.2.cloned.1.call-start
  101.9 1.5 copy.25
  103.4 0.7 reshape.62
  104.1 0.7 broadcast_clamp_fusion
  104.8 6.8 %gather_fusion = f32[1024,2048]{1,0:T(8,128)} fusion(f32[32,2048]{1,0:T(8,128)S(1)} %copy.25, s32[1024]{0:T(1024)S(1)} %broadcast_clamp_fusion), kind=kCustom, calls=%fused_computation | custom fusion | bytes 16781312 | tf_op jit(solution)/shard_map/gather | solution.py:52
  111.6 26.3 %copy.26 = f32[32,32,2048]{1,0,2:T(8,128)} copy(f32[32,32,2048]{2,1,0:T(8,128)} %bitcast.57) | data formatting | bytes 16777216 | tf_op jit(solution)/shard_map/gather | solution.py:52
  137.9 58.1 %fusion.1 = f32[2048,4,32]{2,1,0:T(4,128)} fusion(f32[4,32,2048]{1,0,2:T(4,128)} %copy.27, f32[32,32,2048]{1,0,2:T(8,128)} %copy.26, pred[32,32]{1,0:T(8,128)(4,1)S(1)} %subtract_compare_fusion), kind=kOutput, calls=%fused_computation.6 | convolution fusion | flops 102760448 | bytes 10486784 | tf_op jit(solution)/shard_map/tsc,nsc->ntc/dot_general | solution.py:55
  196.0 8.7 %while.28 = (s32[]{:T(128)}, f32[16,2048]{1,0:T(8,128)S(1)}, s32[]{:T(128)}, f32[8,16,2048]{2,1,0:T(8,128)}, f32[8,16,2048]{2,1,0:T(8,128)}, /*index=5*/s32[]{:T(128)}, s32[]{:T(128)}) while((s32[]{:T(128)}, f32[16,2048]{1,0:T(8,128)S(1)}, s32[]{:T(128)}, f32[8,16,2048]{2,1,0:T(8,128)}, f32[8,16,2048]{2,1,0:T(8,128)}, ...), condition=%wide.region_4.5_spmd.clone, body=%wide.region_3.4_spmd.clone.sunk | while | flops 131076 | bytes 524389 | solution.py:29
  196.0 1.1 fusion.31
  197.1 1.1 fusion.31
  198.2 1.1 fusion.31
  199.3 1.1 fusion.31
  200.4 1.1 fusion.31
  201.5 1.1 fusion.31
  202.6 1.1 fusion.31
  203.7 1.1 fusion.31
  204.8 2.0 multiply_add_fusion
  206.8 4.5 copy.30
  211.3 25.2 %add_bitcast_fusion = f32[4,32,2048]{1,0,2:T(4,128)} fusion(f32[2048,4,32]{2,1,0:T(4,128)} %fusion.1, f32[4,16,2048]{1,0,2:T(4,128)} %copy.30, f32[32]{0:T(128)S(1)} %iota_add_fusion, f32[16,2048]{0,1:T(8,128)} %copy-done.1, f32[16,2048]{0,1:T(8,128)} %copy-done.2), kind=kOutput, calls=%fused_computation.19 | convolution fusion | flops 52690944 | bytes 2883712 | tf_op jit(solution)/shard_map/tmc,nmc->ntc/dot_general | solution.py:77
  236.5 4.6 copy.31
  241.1 2.3 fusion.17
  243.4 171.3 %all-gather.6.cloned.1.call-done = bf16[2048,8192]{1,0:T(8,128)(2,1)} async-done(((bf16[2048,1024]{1,0:T(8,128)(2,1)}), bf16[2048,8192]{1,0:T(8,128)(2,1)}) %all-gather.6.cloned.1.call-update) | async-done | bytes 33554448 | tf_op jit(solution)/shard_map/all_gather | solution.py:82
  414.7 17.3 %fusion.20 = f32[128,8192]{1,0:T(8,128)} fusion(bf16[128,2048]{1,0:T(8,128)(2,1)} %fusion.17, bf16[2048,8192]{1,0:T(8,128)(2,1)} %all-gather.6.cloned.1.call-done), kind=kOutput, calls=%fused_computation.46 | convolution fusion | flops 4294967296 | bytes 38273024 | tf_op jit(solution)/shard_map/dot_general | solution.py:80
  432.0 0.0 reduce-scatter.2.cloned.1.call-update
  432.1 50.1 %reduce-scatter.2.cloned.1.call-done = f32[128,2048]{1,0:T(8,128)} async-done(((f32[128,8192]{1,0:T(8,128)}), f32[128,2048]{1,0:T(8,128)}) %reduce-scatter.2.cloned.1.call-update) | async-done | bytes 1048592 | tf_op jit(solution)/shard_map/reduce_scatter | solution.py:85
  482.2 2.1 convert_element_type.11
  (23 shorter events, 0.1 us)
Async XLA Ops:
  6.5 189.5 %all-gather.8.cloned.1.call-start = ((), (), s32[]{:S(2)}) async-start(), calls=%async_computation.3 | async-start | bytes 1179648 | tf_op jit(solution)/shard_map/all_gather | solution.py:17
  7.5 44.0 %collective-permute-start = (bf16[2,3,2048]{2,0,1:T(2,128)(2,1)S(1)}, bf16[2,3,2048]{2,0,1:T(2,128)(2,1)S(1)}, u32[]{:S(2)}, u32[]{:S(2)}) collective-permute-start(bf16[2,3,2048]{2,0,1:T(2,128)(2,1)S(1)} %slice.31), channel_id=1, source_target_pairs={{0,4},{4,8},{8,12},{12,16},{16,20},{20,24},{24,28},{1,5},{5,9},{9,... | collective-permute-start | bytes 73736 | tf_op jit(solution)/shard_map/ppermute | solution.py:12
  10.9 0.7 copy-start.4
  11.0 185.0 %all-gather.10.cloned.1.call-start = ((), (), s32[]{:S(2)}) async-start(), calls=%async_computation.4 | async-start | bytes 1179648 | tf_op jit(solution)/shard_map/all_gather | solution.py:17
  11.6 14.1 %copy-start.1 = (f32[16,2048]{0,1:T(8,128)}, f32[16,2048]{0,1:T(8,128)S(1)}, u32[]{:S(2)}) copy-start(f32[16,2048]{0,1:T(8,128)S(1)} %copy.24) | copy-start | bytes 393220
  11.9 13.8 %copy-start.2 = (f32[16,2048]{0,1:T(8,128)}, f32[16,2048]{0,1:T(8,128)S(1)}, u32[]{:S(2)}) copy-start(f32[16,2048]{0,1:T(8,128)S(1)} %copy.23) | copy-start | bytes 393220
  11.9 13.8 %copy-start.9 = (f32[3,3,2048]{2,1,0:T(4,128)S(1)}, f32[3,3,2048]{2,1,0:T(4,128)}, u32[]{:S(2)}) copy-start(f32[3,3,2048]{2,1,0:T(4,128)} %param.11) | copy-start | bytes 221188
  26.4 25.1 %copy-start.3 = (bf16[128,3,2048]{2,0,1:T(8,128)(2,1)S(1)}, bf16[128,3,2048]{2,0,1:T(8,128)(2,1)}, u32[]{:S(2)}) copy-start(bf16[128,3,2048]{2,0,1:T(8,128)(2,1)} %param.10) | copy-start | bytes 4718596
  51.5 0.8 copy-start.6
  51.5 0.8 copy-start.7
  51.5 0.8 copy-start.8
  100.2 0.7 copy-start
  100.9 313.8 %all-gather.6.cloned.1.call-start = ((), (), s32[]{:S(2)}) async-start(), calls=%async_computation.1 | async-start | bytes 37748736 | tf_op jit(solution)/shard_map/all_gather | solution.py:82
  101.7 380.5 %reduce-scatter.2.cloned.1.call-start = ((), (), s32[]{:S(2)}) async-start(), calls=%async_computation.2 | async-start | bytes 5242880 | tf_op jit(solution)/shard_map/reduce_scatter | solution.py:85
  137.9 66.8 %copy-start.5 = (f32[16,2048]{1,0:T(8,128)S(1)}, f32[16,2048]{1,0:T(8,128)}, u32[]{:S(2)}) copy-start(f32[16,2048]{1,0:T(8,128)} %copy-done.4) | copy-start | bytes 393220
  236.5 4.6 copy-start.10
Sparse Core Ops, SparseCore 0:
  11.1 23.7 all-gather.7
  101.0 23.7 all-gather.9
  126.4 288.2 all-gather.5
  432.2 49.9 reduce-scatter.1
where the time goes:
time: 495 us; the launch traced here: 491 us
  waiting for transfers between devices  222 us (45%)
  matrix products  131 us (26%)
  local copies, waits for them, and re-layouts  81.9 us (17%)
  other arithmetic  40.3 us (8%)
  between operations  13.3 us (3%)
    all_gather x1, waiting for transfers between devices, shards(): lax.all_gather(out_weight, 'ctx', axis=1, tiled=True)  171 us
    dot_general x1, matrix products, shards(): jnp.einsum('tsc,nsc->ntc', toeplitz, blocks, precision=lax.Precision.HIGH...  58.1 us
    reduce_scatter x1, waiting for transfers between devices, shards(): lax.psum_scatter(partial_sums, 'tp', scatter_dimension=1, tiled=True)  50.1 us
    gather x2, local copies, waits for them, and re-layouts, shards(): kernel[jnp.clip(lag_table, 0, block_len - 1)]  33.1 us
    dot_general x1, matrix products, shards(): jnp.einsum('smc,nsc->nmc', powers[::-1], blocks, precision=lax.Precision....  30.2 us
    dot_general x1, matrix products, shards(): jnp.einsum('tmc,nmc->ntc', after_start, starts, precision=lax.Precision.H...  25.2 us
    rev x1, local copies, waits for them, and re-layouts, shards(): powers[::-1]  25.1 us
    dot_general x1, matrix products, shards(): jnp.dot(gated, lax.all_gather(out_weight, 'ctx', axis=1, tiled=True), pre...  17.3 us
  transfers between devices with their start and end apart: 5, of which 2 were waited for; matrix products, arithmetic and copies ran while one was open for 47% of the time, Pallas kernels for 0%

commit v1 on v0

v1 whole, which is shorter than its diff:
```python
import functools

import jax
import jax.numpy as jnp
from jax import lax
from jax.experimental import pallas as pl
from jax.experimental.pallas import tpu as pltpu
from jax.sharding import PartitionSpec as P

MESH = pl.DeviceIdType.MESH
SEGS = 8
LANES = 128
HALO = 8
TAIL = 16
PARTS = 4


def spread(row):
    return jnp.broadcast_to(row, (SEGS, LANES))


def block_kernel(
    n_ctx, n_tp, x_hbm, taps_hbm, rate_hbm, residue_hbm, skip_hbm, w_hbm, out_ref,
    x_ref, taps_ref, rate_ref, gain_ref, skip_ref, w_ref, load_sem,
    halo_out, halo_in, halo_sem, ext, rows_ref, q_ref, resp_ref, before_ref,
    end_ref, sib_end, chip_end, ends, carry, gbuf, part, pown, psend, prcv, fin, obuf,
    e_send, e_recv, c_send, c_recv, i_send, i_recv, up_sem, dn_sem, g_recv, sib_send, sib_recv,
    p_send, p_recv, f_send, f_recv,
):
    chips = n_ctx // 2
    per = n_ctx // n_tp
    half = n_tp // 2
    _, positions, channels = x_ref.shape
    taps = taps_ref.shape[0]
    modes = rate_ref.shape[0]
    seg = positions // SEGS
    width = channels // PARTS
    columns = w_ref.shape[1]
    share = 2 * positions // n_tp
    c = lax.axis_index("ctx")
    t = lax.axis_index("tp")
    z, core = lax.div(c, 2), lax.rem(c, 2)
    sibling = c + 1 - 2 * core
    mine = (lax.div(c, per) == t) & (core == lax.div(t, half))

    def load(k, src, dst):
        return pltpu.make_async_copy(src, dst, load_sem.at[k])

    loads = [
        load(0, x_hbm, x_ref), load(1, taps_hbm, taps_ref), load(2, rate_hbm, rate_ref),
        load(3, residue_hbm, gain_ref), load(4, skip_hbm, skip_ref), load(5, w_hbm, w_ref),
    ]
    for copy in loads:
        copy.start()

    def at(ctx, tp):
        return {"ctx": ctx, "tp": tp}

    barrier = pltpu.get_barrier_semaphore()

    def greet(ctx, tp):
        pl.semaphore_signal(barrier, inc=1, device_id=at(ctx, tp), device_id_type=MESH)

    @pl.loop(1, n_ctx)
    def _(k):
        greet(lax.rem(c + k, n_ctx), t)

    @pl.loop(1, n_tp)
    def _(k):
        greet(c, lax.rem(t + k, n_tp))

    @pl.loop(0, chips)
    def _(other):
        to_ctx, to_tp = 2 * other + lax.div(t, half), lax.div(c, per)

        @pl.when(~((to_ctx == c) & (to_tp == t)))
        def _():
            greet(to_ctx, to_tp)

    @pl.loop(0, per * half)
    def _(k):
        from_ctx, from_tp = per * t + lax.div(k, half), core * half + lax.rem(k, half)

        @pl.when(~((from_ctx == c) & (from_tp == t)))
        def _():
            greet(from_ctx, from_tp)

    expected = (n_ctx - 1) + (n_tp - 1) + chips + per * half

    @pl.when(mine)
    def _():
        pl.semaphore_wait(barrier, expected - 2)

    @pl.when(~mine)
    def _():
        pl.semaphore_wait(barrier, expected)

    def remote(src, dst, send, recv, ctx, tp):
        return pltpu.make_async_remote_copy(
            src_ref=src, dst_ref=dst, send_sem=send, recv_sem=recv,
            device_id=at(ctx, tp), device_id_type=MESH,
        )

    to_next = remote(halo_out, halo_in, halo_sem.at[0], halo_sem.at[1], c + 1, t)
    for copy in loads[:5]:
        copy.wait()
    for feature in range(3):
        tail = x_ref[feature, pl.ds(positions - TAIL, TAIL), :].astype(jnp.float32)
        halo_out[pl.ds(2 * feature, 2), :] = tail[TAIL - 2 :]
    halo_out[pl.ds(6, 2), :] = jnp.zeros((2, channels), jnp.float32)
    pl.when(c < n_ctx - 1)(lambda: to_next.start())

    twice = -2.0 * rate_ref[...]
    below = jnp.exp(twice) - 1.0
    gain_ref[...] = gain_ref[...] * jnp.sqrt(-(below * twice / jnp.log1p(below)))

    @pl.when(c == 0)
    def _():
        halo_in[...] = jnp.zeros_like(halo_in)

    pl.when(c > 0)(lambda: to_next.wait_recv())

    place = lax.broadcasted_iota(jnp.int32, (SEGS, LANES), 0)
    offset = place.astype(jnp.float32) * float(seg)

    def lanes_of(q, group):
        return pl.ds(pl.multiple_of(q * width + group * LANES, LANES), LANES)

    def scan(q):
        @pl.loop(0, width // LANES)
        def _(group):
            lanes = lanes_of(q, group)
            filtered = []
            for feature in range(3):
                ext[feature, pl.ds(HALO - 2, 2), :] = halo_in[pl.ds(2 * feature, 2), lanes]
                ext[feature, pl.ds(HALO, positions), :] = x_ref[feature, :, lanes].astype(jnp.float32)
                total = taps_ref[0, pl.ds(feature, 1), lanes] * ext[feature, pl.ds(HALO, positions), :]
                for tap in range(1, taps):
                    total += taps_ref[tap, pl.ds(feature, 1), lanes] * ext[feature, pl.ds(HALO - tap, positions), :]
                filtered.append(total)
            rows_ref[0] = filtered[0]
            rows_ref[1] = filtered[1] * filtered[2]
            rate = rate_ref[:, lanes]
            gain = gain_ref[:, lanes]
            decay = jnp.exp(-rate)
            skip = skip_ref[:, lanes]
            decays = [spread(decay[m : m + 1]) for m in range(modes)]
            gains = [spread(gain[m : m + 1]) for m in range(modes)]
            states = [jnp.zeros((SEGS, LANES), jnp.float32)] * modes
            for i in range(seg):
                drive = rows_ref[1, pl.ds(i, SEGS, stride=seg), :]
                response = skip * drive
                for m in range(modes):
                    states[m] = decays[m] * states[m] + drive
                    response = response + gains[m] * states[m]
                resp_ref[i, :, lanes] = response
                q_ref[i, :, lanes] = rows_ref[0, pl.ds(i, SEGS, stride=seg), :]
            powers = [jnp.exp(-rate * float(seg * k)) for k in (1, 2, 4)]
            inside = pl.ds(pl.multiple_of(group * LANES, LANES), LANES)
            for m in range(modes):
                state = states[m]
                for k, power in zip((1, 2, 4), powers):
                    state = state + jnp.where(place >= k, spread(power[m : m + 1]) * pltpu.roll(state, k, 0), 0.0)
                before_ref[m, :, lanes] = jnp.where(place >= 1, pltpu.roll(state, 1, 0), 0.0)
                end_ref[q, pl.ds(m, 1), inside] = state[SEGS - 1 :]

    def to_core1(q):
        return remote(end_ref.at[q], sib_end.at[q], e_send.at[q], e_recv.at[q], sibling, t)

    def to_core0(q):
        return remote(carry.at[q], carry.at[q], i_send.at[q], i_recv.at[q], sibling, t)

    def to_chip(other, q):
        return remote(chip_end.at[q], ends.at[z, q], c_send.at[other, q], c_recv.at[z, q], 2 * other + 1, t)

    def from_chip(other, q):
        return remote(chip_end.at[q], ends.at[other, q], c_send.at[other, q], c_recv.at[other, q], 2 * z + 1, t)

    def decay_over(q, steps):
        return jnp.exp(rate_ref[:, pl.ds(pl.multiple_of(q * width, LANES), width)] * -float(steps))

    def pair(q):
        @pl.when(core == 1)
        def _():
            to_core1(q).wait_recv()
            chip_end[q] = decay_over(q, positions) * sib_end[q] + end_ref[q]

            @pl.loop(z + 1, chips)
            def _(other):
                to_chip(other, q).start()

    def receive(q):
        @pl.when(core == 0)
        def _():
            @pl.when(z > 0)
            def _():
                to_core0(q).wait_recv()

            @pl.when(z == 0)
            def _():
                carry[q] = jnp.zeros_like(carry[q])

        @pl.when(core == 1)
        def _():
            carry[q] = jnp.zeros_like(carry[q])

            @pl.loop(0, z)
            def _(other):
                from_chip(other, q).wait_recv()
                carry[q] = decay_over(q, 2 * positions) * carry[q] + ends[other, q]

            @pl.when(z > 0)
            def _():
                to_core0(q).start()
                to_core0(q).wait_send()

            carry[q] = decay_over(q, positions) * carry[q] + sib_end[q]

    def gate(q):
        @pl.loop(0, width // LANES)
        def _(group):
            lanes = lanes_of(q, group)
            inside = pl.ds(pl.multiple_of(group * LANES, LANES), LANES)
            rate = rate_ref[:, lanes]
            gain = gain_ref[:, lanes]
            decay = jnp.exp(-rate)
            incoming = carry[q, :, inside]
            values, decays = [], []
            for m in range(modes):
                lead = jnp.exp(-rate[m : m + 1] * offset)
                values.append(gain[m : m + 1] * (before_ref[m, :, lanes] + lead * incoming[m : m + 1]))
                decays.append(spread(decay[m : m + 1]))
            for i in range(seg):
                response = resp_ref[i, :, lanes]
                for m in range(modes):
                    values[m] = decays[m] * values[m]
                    response = response + values[m]
                rows_ref[0, pl.ds(i, SEGS, stride=seg), :] = q_ref[i, :, lanes] * response
            gbuf[z, core, q, :, inside] = rows_ref[0].astype(jnp.bfloat16)

    def g_copy(other, q, sems, ctx):
        block = gbuf.at[other, core, q]
        return remote(block, block, sems.at[other, q], g_recv.at[other, q], ctx, t)

    def go_up(other, q):
        return g_copy(other, q, up_sem, c + 2)

    def go_down(other, q):
        return g_copy(other, q, dn_sem, c - 2)

    def to_sibling(other, q):
        block = gbuf.at[other, core, q]
        return remote(block, block, sib_send.at[other, q], sib_recv.at[other, q], sibling, t)

    def from_sibling(other, q):
        block = gbuf.at[other, 1 - core, q]
        return remote(block, block, sib_send.at[other, q], sib_recv.at[other, q], sibling, t)

    def p_copy(other, k):
        to_tp = lax.rem(t + k, n_tp)
        return remote(
            psend.at[other, to_tp], prcv.at[other, k - 1], p_send.at[other, k - 1], p_recv.at[other, k - 1], c, to_tp
        )

    row0 = pl.multiple_of(lax.rem(t, half) * share, share)
    col0 = pl.multiple_of(lax.rem(c, per) * columns, columns)

    def home(other):
        return remote(
            fin.at[other], obuf.at[pl.ds(row0, share), pl.ds(col0, columns)], f_send.at[other],
            f_recv.at[lax.rem(c, per) * half + lax.rem(t, half)], 2 * other + lax.div(t, half), lax.div(c, per),
        )

    def is_home(other):
        return (2 * other + lax.div(t, half) == c) & (lax.div(c, per) == t)

    tile = min(256, columns)

    def multiply(other, q):
        from_sibling(other, q).wait_recv()
        rows = gbuf[other, :, q].reshape(2 * positions, width)
        depth = pl.ds(pl.multiple_of(q * width, width), width)

        @pl.loop(0, columns // tile)
        def _(j):
            cols = pl.ds(pl.multiple_of(j * tile, tile), tile)
            product = jnp.dot(rows, w_ref[depth, cols], preferred_element_type=jnp.float32)

            @pl.when(q == 0)
            def _():
                part[other, :, cols] = product

            @pl.when(q > 0)
            def _():
                part[other, :, cols] = part[other, :, cols] + product

    def share_out(other):
        @pl.loop(1, n_tp)
        def _(k):
            to_tp = lax.rem(t + k, n_tp)
            rows = pl.ds(pl.multiple_of(to_tp * share, share), share)
            psend[other, to_tp] = part[other, rows, :].astype(jnp.bfloat16)
            p_copy(other, k).start()

    def finish(other):
        pown[...] = part[other, pl.ds(pl.multiple_of(t * share, share), share), :]

        @pl.loop(1, n_tp)
        def _(k):
            p_copy(other, k).wait_recv()
            pown[...] = pown[...] + prcv[other, k - 1].astype(jnp.float32)

        fin[other] = pown[...].astype(jnp.bfloat16)

        @pl.when(is_home(other))
        def _():
            obuf[pl.ds(row0, share), pl.ds(col0, columns)] = fin[other]

        @pl.when(~is_home(other))
        def _():
            home(other).start()

    def sides(d, work):
        for side in range(2):
            other = z - d if side == 0 else z + d
            valid = (other >= 0) if side == 0 else ((other < chips) & (d > 0))
            pl.when(valid)(functools.partial(work, other, side))

    def arrive(q, other, side):
        g_copy(other, q, up_sem, c).wait_recv()
        if side == 0:
            pl.when(z < chips - 1)(lambda: go_up(other, q).start())
        else:
            pl.when(z > 0)(lambda: go_down(other, q).start())
        to_sibling(other, q).start()

    @pl.loop(0, PARTS)
    def _(q):
        scan(q)
        pl.when(core == 0)(lambda: to_core1(q).start())
        pl.when(q > 0)(lambda: pair(q - 1))

    pair(PARTS - 1)

    @pl.loop(0, PARTS)
    def _(q):
        receive(q)
        gate(q)
        pl.when(z < chips - 1)(lambda: go_up(z, q).start())
        pl.when(z > 0)(lambda: go_down(z, q).start())
        to_sibling(z, q).start()

    loads[5].wait()

    @pl.loop(0, PARTS)
    def _(q):
        multiply(z, q)

    share_out(z)

    @pl.loop(1, chips)
    def _(d):
        @pl.loop(0, PARTS)
        def _(q):
            sides(d, functools.partial(arrive, q))
            sides(d, lambda other, side: multiply(other, q))
            pl.when(q == PARTS // 2 - 1)(lambda: sides(d - 1, lambda other, side: finish(other)))

        sides(d, lambda other, side: share_out(other))

    sides(chips - 1, lambda other, side: finish(other))

    @pl.loop(0, per * half)
    def _(k):
        from_ctx, from_tp = per * t + lax.div(k, half), core * half + lax.rem(k, half)

        @pl.when(~((from_ctx == c) & (from_tp == t)))
        def _():
            rows = pl.multiple_of(lax.rem(k, half) * share, share)
            cols = pl.multiple_of(lax.div(k, half) * columns, columns)
            block = obuf.at[pl.ds(rows, share), pl.ds(cols, columns)]
            remote(fin.at[0], block, f_send.at[0], f_recv.at[k], from_ctx, from_tp).wait_recv()

    out_ref[...] = obuf[...]

    pl.when(c < n_ctx - 1)(lambda: to_next.wait_send())

    @pl.loop(0, PARTS)
    def _(q):
        pl.when(core == 0)(lambda: to_core1(q).wait_send())

        @pl.when(core == 1)
        def _():
            @pl.loop(z + 1, chips)
            def _(other):
                to_chip(other, q).wait_send()

        @pl.loop(0, chips)
        def _(other):
            pl.when((z < chips - 1) & (other <= z))(lambda: go_up(other, q).wait_send())
            pl.when((z > 0) & (other >= z))(lambda: go_down(other, q).wait_send())
            to_sibling(other, q).wait_send()

    @pl.loop(0, chips)
    def _(other):
        @pl.loop(1, n_tp)
        def _(k):
            p_copy(other, k).wait_send()

        pl.when(~is_home(other))(lambda: home(other).wait_send())


def block(n_ctx, n_tp, x, taps, rate, residue, skip, w):
    _, positions, channels = x.shape
    modes = rate.shape[0]
    seg = positions // SEGS
    width = channels // PARTS
    columns = w.shape[1]
    chips = n_ctx // 2
    share = 2 * positions // n_tp
    out_cols = columns * (n_ctx // n_tp)
    f32, bf16, dma = jnp.float32, jnp.bfloat16, pltpu.SemaphoreType.DMA
    return pl.pallas_call(
        functools.partial(block_kernel, n_ctx, n_tp),
        out_shape=jax.ShapeDtypeStruct((positions, out_cols), bf16),
        in_specs=[pl.BlockSpec(memory_space=pltpu.HBM)] * 6,
        out_specs=pl.BlockSpec(memory_space=pltpu.VMEM),
        scratch_shapes=[
            pltpu.VMEM(x.shape, bf16),
            pltpu.VMEM(taps.shape, f32),
            pltpu.VMEM((modes, channels), f32),
            pltpu.VMEM((modes, channels), f32),
            pltpu.VMEM((1, channels), f32),
            pltpu.VMEM(w.shape, bf16),
            dma((6,)),
            pltpu.VMEM((8, channels), f32),
            pltpu.VMEM((8, channels), f32),
            dma((2,)),
            pltpu.VMEM((3, HALO + positions, LANES), f32),
            pltpu.VMEM((2, positions, LANES), f32),
            pltpu.VMEM((seg, SEGS, channels), f32),
            pltpu.VMEM((seg, SEGS, channels), f32),
            pltpu.VMEM((modes, SEGS, channels), f32),
            pltpu.VMEM((PARTS, modes, width), f32),
            pltpu.VMEM((PARTS, modes, width), f32),
            pltpu.VMEM((PARTS, modes, width), f32),
            pltpu.VMEM((chips, PARTS, modes, width), f32),
            pltpu.VMEM((PARTS, modes, width), f32),
            pltpu.VMEM((chips, 2, PARTS, positions, width), bf16),
            pltpu.VMEM((chips, 2 * positions, columns), f32),
            pltpu.VMEM((share, columns), f32),
            pltpu.VMEM((chips, n_tp, share, columns), bf16),
            pltpu.VMEM((chips, n_tp - 1, share, columns), bf16),
            pltpu.VMEM((chips, share, columns), bf16),
            pltpu.VMEM((positions, out_cols), bf16),
            dma((PARTS,)),
            dma((PARTS,)),
            dma((chips, PARTS)),
            dma((chips, PARTS)),
            dma((PARTS,)),
            dma((PARTS,)),
            dma((chips, PARTS)),
            dma((chips, PARTS)),
            dma((chips, PARTS)),
            dma((chips, PARTS)),
            dma((chips, PARTS)),
            dma((chips, n_tp - 1)),
            dma((chips, n_tp - 1)),
            dma((chips,)),
            dma((n_ctx // n_tp * (n_tp // 2),)),
        ],
        compiler_params=pltpu.CompilerParams(
            collective_id=0, has_side_effects=True, vmem_limit_bytes=60 * 1024 * 1024
        ),
        name="block",
    )(x, taps, rate, residue, skip, w)


def solution(mesh):
    n_ctx, n_tp = mesh.shape["ctx"], mesh.shape["tp"]

    def shards(features, short_filter, decay_rate, residue, skip, out_weight):
        x = jnp.transpose(features, (1, 0, 2))
        return block(n_ctx, n_tp, x, short_filter, decay_rate, residue, skip[None], out_weight)

    in_specs = (
        P("ctx", None, "tp"),
        P(None, None, "tp"),
        P(None, "tp"),
        P(None, "tp"),
        P("tp"),
        P("tp", "ctx"),
    )
    return jax.shard_map(shards, mesh=mesh, in_specs=in_specs, out_specs=P("ctx", "tp"), check_vma=False)
```

time: 495 us -> 89.3 us (0.18)
  waiting for transfers between devices: 222 us -> 0 us
  matrix products: 131 us -> 0 us
  Pallas kernels: 0 us -> 87.3 us
  local copies, waits for them, and re-layouts: 81.9 us -> 1.88 us
  other arithmetic: 40.3 us -> 0 us
  between operations: 13.3 us -> 0.01 us
    all_gather x3 -> x0, waiting for transfers between devices: 171 us -> none  [the longest x1 171 us: shards(): lax.all_gather(out_weight, 'ctx', axis=1, tiled=True)]
    dot_general x4 -> x0, matrix products: 131 us -> none  [the longest x1 58.1 us: shards(): jnp.einsum('tsc,nsc->ntc', toeplitz, blocks, precision=lax.Precision.HIGH...]
    pallas_call x0 -> x1, Pallas kernels: none -> 87.3 us  [block(): pl.pallas_call(functools.partial(block_kernel, n_ctx, n_tp), out_shape=ja...]
    reduce_scatter x1 -> x0, waiting for transfers between devices: 50.1 us -> none  [shards(): lax.psum_scatter(partial_sums, 'tp', scatter_dimension=1, tiled=True)]
    gather x2 -> x0, local copies, waits for them, and re-layouts: 33.1 us -> none  [shards(): kernel[jnp.clip(lag_table, 0, block_len - 1)]]
    rev x1 -> x0, local copies, waits for them, and re-layouts: 25.1 us -> none  [shards(): powers[::-1]]
    exp x2 -> x0, other arithmetic: 15.5 us -> none  [the longest x1 13.8 us: shards(): powers = jnp.exp(-decay_rate[None] * offsets[:, None, None])]
    add x2 -> x0, local copies, waits for them, and re-layouts: 9.09 us -> none  [the longest x1 4.57 us: shards(): inside + carried]
  transfers between devices with their start and end apart: 5 -> 0, of which waited for: 2 -> 0; matrix products, arithmetic and copies ran while one was open for 47% -> 0% of each run, Pallas kernels for 0% -> 0%
where the time goes in v1:
time: 89.3 us; the launch traced here: 89.2 us
  Pallas kernels  87.3 us (98%)
  local copies, waits for them, and re-layouts  1.88 us (2%)
    pallas_call x1, Pallas kernels, block(): pl.pallas_call(functools.partial(block_kernel, n_ctx, n_tp), out_shape=ja...  87.3 us
    unnamed x1, local copies, waits for them, and re-layouts  1.88 us

profile of v1, /device:TPU:6, one launch (start us, length us, event | category | flops | bytes accessed | tf_op | source)
XLA Modules:
  0.0 89.2 jit_solution(7060304965333902532)
XLA Ops:
  0.0 87.3 %block.1 = bf16[128,2048]{1,0:T(8,128)(2,1)} custom-call(bf16[3,128,2048]{2,1,0:T(8,128)(2,1)} %bitcast.2, f32[3,3,2048]{2,1,0:T(4,128)} %taps_hbm.1, f32[16,2048]{1,0:T(8,128)} %rate_hbm.1, f32[16,2048]{1,0:T(8,128)} %residue_hbm.1, f32[1,2048]{1,0:T(1,128)} %bitcast.3, bf16[2048,1024]{1,0:T(8,128)(2,1)} %w_hbm.1), custom_call_target="tpu_custom_call" | custom-call | tf_op jit(solution)/shard_map/block/pallas_call | solution.py:423
  87.3 1.9 %copy.8 = bf16[128,2048]{1,0:T(8,128)(2,1)} copy(bf16[128,2048]{1,0:T(8,128)(2,1)} %block.1) | data formatting | bytes 1048576

commit v2 on v1

--- a/solution.py
+++ b/solution.py
@@ -12,7 +12,7 @@
 LANES = 128
 HALO = 8
 TAIL = 16
-PARTS = 4
+PARTS = 8
 
 
 def spread(row):
@@ -23,19 +23,22 @@
     n_ctx, n_tp, x_hbm, taps_hbm, rate_hbm, residue_hbm, skip_hbm, w_hbm, out_ref,
     x_ref, taps_ref, rate_ref, gain_ref, skip_ref, w_ref, load_sem,
     halo_out, halo_in, halo_sem, ext, rows_ref, q_ref, resp_ref, before_ref,
-    end_ref, sib_end, chip_end, ends, carry, gbuf, part, pown, psend, prcv, fin, obuf,
+    end_ref, sib_end, chip_end, chip_in, ends, carry, gbuf, part, pown, psend, prcv, fin, obuf,
     e_send, e_recv, c_send, c_recv, i_send, i_recv, up_sem, dn_sem, g_recv, sib_send, sib_recv,
     p_send, p_recv, f_send, f_recv,
 ):
     chips = n_ctx // 2
+    parts = end_ref.shape[0]
+    delay = max(1, parts // 2)
     per = n_ctx // n_tp
     half = n_tp // 2
     _, positions, channels = x_ref.shape
     taps = taps_ref.shape[0]
     modes = rate_ref.shape[0]
     seg = positions // SEGS
-    width = channels // PARTS
+    width = channels // parts
     columns = w_ref.shape[1]
+    wide = columns // 2
     share = 2 * positions // n_tp
     c = lax.axis_index("ctx")
     t = lax.axis_index("tp")
@@ -168,7 +171,7 @@
         return remote(end_ref.at[q], sib_end.at[q], e_send.at[q], e_recv.at[q], sibling, t)
 
     def to_core0(q):
-        return remote(carry.at[q], carry.at[q], i_send.at[q], i_recv.at[q], sibling, t)
+        return remote(chip_in.at[q], carry.at[q], i_send.at[q], i_recv.at[q], sibling, t)
 
     def to_chip(other, q):
         return remote(chip_end.at[q], ends.at[z, q], c_send.at[other, q], c_recv.at[z, q], 2 * other + 1, t)
@@ -202,19 +205,15 @@
 
         @pl.when(core == 1)
         def _():
-            carry[q] = jnp.zeros_like(carry[q])
+            chip_in[q] = jnp.zeros_like(chip_in[q])
 
             @pl.loop(0, z)
             def _(other):
                 from_chip(other, q).wait_recv()
-                carry[q] = decay_over(q, 2 * positions) * carry[q] + ends[other, q]
-
-            @pl.when(z > 0)
-            def _():
-                to_core0(q).start()
-                to_core0(q).wait_send()
-
-            carry[q] = decay_over(q, positions) * carry[q] + sib_end[q]
+                chip_in[q] = decay_over(q, 2 * positions) * chip_in[q] + ends[other, q]
+
+            pl.when(z > 0)(lambda: to_core0(q).start())
+            carry[q] = decay_over(q, positions) * chip_in[q] + sib_end[q]
 
     def gate(q):
         @pl.loop(0, width // LANES)
@@ -256,19 +255,20 @@
         block = gbuf.at[other, 1 - core, q]
         return remote(block, block, sib_send.at[other, q], sib_recv.at[other, q], sibling, t)
 
-    def p_copy(other, k):
+    def p_copy(other, k, h):
         to_tp = lax.rem(t + k, n_tp)
         return remote(
-            psend.at[other, to_tp], prcv.at[other, k - 1], p_send.at[other, k - 1], p_recv.at[other, k - 1], c, to_tp
+            psend.at[other, to_tp, h], prcv.at[other, k - 1, h], p_send.at[other, k - 1, h],
+            p_recv.at[other, k - 1, h], c, to_tp,
         )
 
     row0 = pl.multiple_of(lax.rem(t, half) * share, share)
     col0 = pl.multiple_of(lax.rem(c, per) * columns, columns)
 
-    def home(other):
+    def home(other, h):
         return remote(
-            fin.at[other], obuf.at[pl.ds(row0, share), pl.ds(col0, columns)], f_send.at[other],
-            f_recv.at[lax.rem(c, per) * half + lax.rem(t, half)], 2 * other + lax.div(t, half), lax.div(c, per),
+            fin.at[other, h], obuf.at[pl.ds(row0, share), pl.ds(col0 + h * wide, wide)], f_send.at[other, h],
+            f_recv.at[lax.rem(c, per) * half + lax.rem(t, half), h], 2 * other + lax.div(t, half), lax.div(c, per),
         )
 
     def is_home(other):
@@ -295,30 +295,32 @@
                 part[other, :, cols] = part[other, :, cols] + product
 
     def share_out(other):
-        @pl.loop(1, n_tp)
-        def _(k):
-            to_tp = lax.rem(t + k, n_tp)
-            rows = pl.ds(pl.multiple_of(to_tp * share, share), share)
-            psend[other, to_tp] = part[other, rows, :].astype(jnp.bfloat16)
-            p_copy(other, k).start()
+        for h in range(2):
+            @pl.loop(1, n_tp)
+            def _(k):
+                to_tp = lax.rem(t + k, n_tp)
+                rows = pl.ds(pl.multiple_of(to_tp * share, share), share)
+                psend[other, to_tp, h] = part[other, rows, pl.ds(h * wide, wide)].astype(jnp.bfloat16)
+                p_copy(other, k, h).start()
 
     def finish(other):
-        pown[...] = part[other, pl.ds(pl.multiple_of(t * share, share), share), :]
-
-        @pl.loop(1, n_tp)
-        def _(k):
-            p_copy(other, k).wait_recv()
-            pown[...] = pown[...] + prcv[other, k - 1].astype(jnp.float32)
-
-        fin[other] = pown[...].astype(jnp.bfloat16)
-
-        @pl.when(is_home(other))
-        def _():
-            obuf[pl.ds(row0, share), pl.ds(col0, columns)] = fin[other]
-
-        @pl.when(~is_home(other))
-        def _():
-            home(other).start()
+        for h in range(2):
+            pown[...] = part[other, pl.ds(pl.multiple_of(t * share, share), share), pl.ds(h * wide, wide)]
+
+            @pl.loop(1, n_tp)
+            def _(k):
+                p_copy(other, k, h).wait_recv()
+                pown[...] = pown[...] + prcv[other, k - 1, h].astype(jnp.float32)
+
+            fin[other, h] = pown[...].astype(jnp.bfloat16)
+
+            @pl.when(is_home(other))
+            def _():
+                obuf[pl.ds(row0, share), pl.ds(col0 + h * wide, wide)] = fin[other, h]
+
+            @pl.when(~is_home(other))
+            def _():
+                home(other, h).start()
 
     def sides(d, work):
         for side in range(2):
@@ -334,25 +336,29 @@
             pl.when(z > 0)(lambda: go_down(other, q).start())
         to_sibling(other, q).start()
 
-    @pl.loop(0, PARTS)
-    def _(q):
-        scan(q)
-        pl.when(core == 0)(lambda: to_core1(q).start())
-        pl.when(q > 0)(lambda: pair(q - 1))
-
-    pair(PARTS - 1)
-
-    @pl.loop(0, PARTS)
-    def _(q):
-        receive(q)
-        gate(q)
-        pl.when(z < chips - 1)(lambda: go_up(z, q).start())
-        pl.when(z > 0)(lambda: go_down(z, q).start())
-        to_sibling(z, q).start()
+    late = jnp.where(z == 0, core, delay)
+
+    @pl.loop(0, parts + delay)
+    def _(step):
+        @pl.when(step < parts)
+        def _():
+            scan(step)
+            pl.when(core == 0)(lambda: to_core1(step).start())
+
+        pl.when((step > 0) & (step <= parts))(lambda: pair(step - 1))
+        q = step - late
+
+        @pl.when((q >= 0) & (q < parts))
+        def _():
+            receive(q)
+            gate(q)
+            pl.when(z < chips - 1)(lambda: go_up(z, q).start())
+            pl.when(z > 0)(lambda: go_down(z, q).start())
+            to_sibling(z, q).start()
 
     loads[5].wait()
 
-    @pl.loop(0, PARTS)
+    @pl.loop(0, parts)
     def _(q):
         multiply(z, q)
 
@@ -360,11 +366,11 @@
 
     @pl.loop(1, chips)
     def _(d):
-        @pl.loop(0, PARTS)
+        @pl.loop(0, parts)
         def _(q):
             sides(d, functools.partial(arrive, q))
             sides(d, lambda other, side: multiply(other, q))
-            pl.when(q == PARTS // 2 - 1)(lambda: sides(d - 1, lambda other, side: finish(other)))
+            pl.when(q == parts // 2 - 1)(lambda: sides(d - 1, lambda other, side: finish(other)))
 
         sides(d, lambda other, side: share_out(other))
 
@@ -378,19 +384,22 @@
         def _():
             rows = pl.multiple_of(lax.rem(k, half) * share, share)
             cols = pl.multiple_of(lax.div(k, half) * columns, columns)
-            block = obuf.at[pl.ds(rows, share), pl.ds(cols, columns)]
-            remote(fin.at[0], block, f_send.at[0], f_recv.at[k], from_ctx, from_tp).wait_recv()
+            for h in range(2):
+                block = obuf.at[pl.ds(rows, share), pl.ds(cols + h * wide, wide)]
+                remote(fin.at[0, h], block, f_send.at[0, h], f_recv.at[k, h], from_ctx, from_tp).wait_recv()
 
     out_ref[...] = obuf[...]
 
     pl.when(c < n_ctx - 1)(lambda: to_next.wait_send())
 
-    @pl.loop(0, PARTS)
+    @pl.loop(0, parts)
     def _(q):
         pl.when(core == 0)(lambda: to_core1(q).wait_send())
 
         @pl.when(core == 1)
         def _():
+            pl.when(z > 0)(lambda: to_core0(q).wait_send())
+
             @pl.loop(z + 1, chips)
             def _(other):
                 to_chip(other, q).wait_send()
@@ -405,16 +414,21 @@
     def _(other):
         @pl.loop(1, n_tp)
         def _(k):
-            p_copy(other, k).wait_send()
-
-        pl.when(~is_home(other))(lambda: home(other).wait_send())
+            for h in range(2):
+                p_copy(other, k, h).wait_send()
+
+        @pl.when(~is_home(other))
+        def _():
+            for h in range(2):
+                home(other, h).wait_send()
 
 
 def block(n_ctx, n_tp, x, taps, rate, residue, skip, w):
     _, positions, channels = x.shape
     modes = rate.shape[0]
     seg = positions // SEGS
-    width = channels // PARTS
+    parts = min(PARTS, channels // LANES)
+    width = channels // parts
     columns = w.shape[1]
     chips = n_ctx // 2
     share = 2 * positions // n_tp
@@ -441,33 +455,34 @@
             pltpu.VMEM((seg, SEGS, channels), f32),
             pltpu.VMEM((seg, SEGS, channels), f32),
             pltpu.VMEM((modes, SEGS, channels), f32),
-            pltpu.VMEM((PARTS, modes, width), f32),
-            pltpu.VMEM((PARTS, modes, width), f32),
-            pltpu.VMEM((PARTS, modes, width), f32),
-            pltpu.VMEM((chips, PARTS, modes, width), f32),
-            pltpu.VMEM((PARTS, modes, width), f32),
-            pltpu.VMEM((chips, 2, PARTS, positions, width), bf16),
+            pltpu.VMEM((parts, modes, width), f32),
+            pltpu.VMEM((parts, modes, width), f32),
+            pltpu.VMEM((parts, modes, width), f32),
+            pltpu.VMEM((parts, modes, width), f32),
+            pltpu.VMEM((chips, parts, modes, width), f32),
+            pltpu.VMEM((parts, modes, width), f32),
+            pltpu.VMEM((chips, 2, parts, positions, width), bf16),
             pltpu.VMEM((chips, 2 * positions, columns), f32),
-            pltpu.VMEM((share, columns), f32),
-            pltpu.VMEM((chips, n_tp, share, columns), bf16),
-            pltpu.VMEM((chips, n_tp - 1, share, columns), bf16),
-            pltpu.VMEM((chips, share, columns), bf16),
+            pltpu.VMEM((share, columns // 2), f32),
+            pltpu.VMEM((chips, n_tp, 2, share, columns // 2), bf16),
+            pltpu.VMEM((chips, n_tp - 1, 2, share, columns // 2), bf16),
+            pltpu.VMEM((chips, 2, share, columns // 2), bf16),
             pltpu.VMEM((positions, out_cols), bf16),
-            dma((PARTS,)),
-            dma((PARTS,)),
-            dma((chips, PARTS)),
-            dma((chips, PARTS)),
-            dma((PARTS,)),
-            dma((PARTS,)),
-            dma((chips, PARTS)),
-            dma((chips, PARTS)),
-            dma((chips, PARTS)),
-            dma((chips, PARTS)),
-            dma((chips, PARTS)),
-            dma((chips, n_tp - 1)),
-            dma((chips, n_tp - 1)),
-            dma((chips,)),
-            dma((n_ctx // n_tp * (n_tp // 2),)),
+            dma((parts,)),
+            dma((parts,)),
+            dma((chips, parts)),
+            dma((chips, parts)),
+            dma((parts,)),
+            dma((parts,)),
+            dma((chips, parts)),
+            dma((chips, parts)),
+            dma((chips, parts)),
+            dma((chips, parts)),
+            dma((chips, parts)),
+            dma((chips, n_tp - 1, 2)),
+            dma((chips, n_tp - 1, 2)),
+            dma((chips, 2)),
+            dma((n_ctx // n_tp * (n_tp // 2), 2)),
         ],
         compiler_params=pltpu.CompilerParams(
             collective_id=0, has_side_effects=True, vmem_limit_bytes=60 * 1024 * 1024

time: 89.3 us -> 107 us (1.20)
  Pallas kernels: 87.3 us -> 105 us
    pallas_call x1, Pallas kernels: 87.3 us -> 105 us  [block(): pl.pallas_call(functools.partial(block_kernel, n_ctx, n_tp), out_shape=ja...]
where the time goes in v2:
time: 107 us
  Pallas kernels  105 us (98%)
  local copies, waits for them, and re-layouts  1.88 us (2%)
    pallas_call x1, Pallas kernels, block(): pl.pallas_call(functools.partial(block_kernel, n_ctx, n_tp), out_shape=ja...  105 us

profile of v2, /device:TPU:6, one launch (start us, length us, event | category | flops | bytes accessed | tf_op | source)
XLA Modules:
  0.0 106.7 jit_solution(6103780164099748234)
XLA Ops:
  0.0 104.8 %block.1 = bf16[128,2048]{1,0:T(8,128)(2,1)} custom-call(bf16[3,128,2048]{2,1,0:T(8,128)(2,1)} %bitcast.2, f32[3,3,2048]{2,1,0:T(4,128)} %taps_hbm.1, f32[16,2048]{1,0:T(8,128)} %rate_hbm.1, f32[16,2048]{1,0:T(8,128)} %residue_hbm.1, f32[1,2048]{1,0:T(1,128)} %bitcast.3, bf16[2048,1024]{1,0:T(8,128)(2,1)} %w_hbm.1), custom_call_target="tpu_custom_call" | custom-call | tf_op jit(solution)/shard_map/block/pallas_call | solution.py:437
  104.8 1.9 %copy.8 = bf16[128,2048]{1,0:T(8,128)(2,1)} copy(bf16[128,2048]{1,0:T(8,128)(2,1)} %block.1) | data formatting | bytes 1048576

commit v3 on v2

--- a/solution.py
+++ b/solution.py
@@ -12,7 +12,7 @@
 LANES = 128
 HALO = 8
 TAIL = 16
-PARTS = 8
+PARTS = 4
 
 
 def spread(row):
@@ -21,7 +21,7 @@
 
 def block_kernel(
     n_ctx, n_tp, x_hbm, taps_hbm, rate_hbm, residue_hbm, skip_hbm, w_hbm, out_ref,
-    x_ref, taps_ref, rate_ref, gain_ref, skip_ref, w_ref, load_sem,
+    x_ref, taps_ref, rate_ref, decay_ref, gain_ref, skip_ref, w_ref, load_sem,
     halo_out, halo_in, halo_sem, ext, rows_ref, q_ref, resp_ref, before_ref,
     end_ref, sib_end, chip_end, chip_in, ends, carry, gbuf, part, pown, psend, prcv, fin, obuf,
     e_send, e_recv, c_send, c_recv, i_send, i_recv, up_sem, dn_sem, g_recv, sib_send, sib_recv,
@@ -115,6 +115,7 @@
 
     twice = -2.0 * rate_ref[...]
     below = jnp.exp(twice) - 1.0
+    decay_ref[...] = jnp.exp(rate_ref[...] * -float(positions))
     gain_ref[...] = gain_ref[...] * jnp.sqrt(-(below * twice / jnp.log1p(below)))
 
     @pl.when(c == 0)
@@ -179,14 +180,14 @@
     def from_chip(other, q):
         return remote(chip_end.at[q], ends.at[other, q], c_send.at[other, q], c_recv.at[other, q], 2 * z + 1, t)
 
-    def decay_over(q, steps):
-        return jnp.exp(rate_ref[:, pl.ds(pl.multiple_of(q * width, LANES), width)] * -float(steps))
+    def device_decay(q):
+        return decay_ref[:, pl.ds(pl.multiple_of(q * width, LANES), width)]
 
     def pair(q):
         @pl.when(core == 1)
         def _():
             to_core1(q).wait_recv()
-            chip_end[q] = decay_over(q, positions) * sib_end[q] + end_ref[q]
+            chip_end[q] = device_decay(q) * sib_end[q] + end_ref[q]
 
             @pl.loop(z + 1, chips)
             def _(other):
@@ -210,10 +211,10 @@
             @pl.loop(0, z)
             def _(other):
                 from_chip(other, q).wait_recv()
-                chip_in[q] = decay_over(q, 2 * positions) * chip_in[q] + ends[other, q]
+                chip_in[q] = (device_decay(q) * device_decay(q)) * chip_in[q] + ends[other, q]
 
             pl.when(z > 0)(lambda: to_core0(q).start())
-            carry[q] = decay_over(q, positions) * chip_in[q] + sib_end[q]
+            carry[q] = device_decay(q) * chip_in[q] + sib_end[q]
 
     def gate(q):
         @pl.loop(0, width // LANES)
@@ -276,23 +277,16 @@
 
     tile = min(256, columns)
 
-    def multiply(other, q):
-        from_sibling(other, q).wait_recv()
-        rows = gbuf[other, :, q].reshape(2 * positions, width)
-        depth = pl.ds(pl.multiple_of(q * width, width), width)
-
-        @pl.loop(0, columns // tile)
-        def _(j):
-            cols = pl.ds(pl.multiple_of(j * tile, tile), tile)
+    def multiply(other, first):
+        chunks = range(parts // 2) if first else range(parts // 2, parts)
+        for q in chunks:
+            from_sibling(other, q).wait_recv()
+        rows = jnp.concatenate([gbuf[other, :, q].reshape(2 * positions, width) for q in chunks], axis=1)
+        depth = pl.ds(chunks[0] * width, len(chunks) * width)
+        for j in range(columns // tile):
+            cols = pl.ds(j * tile, tile)
             product = jnp.dot(rows, w_ref[depth, cols], preferred_element_type=jnp.float32)
-
-            @pl.when(q == 0)
-            def _():
-                part[other, :, cols] = product
-
-            @pl.when(q > 0)
-            def _():
-                part[other, :, cols] = part[other, :, cols] + product
+            part[other, :, cols] = product if first else part[other, :, cols] + product
 
     def share_out(other):
         for h in range(2):
@@ -358,21 +352,27 @@
 
     loads[5].wait()
 
-    @pl.loop(0, parts)
-    def _(q):
-        multiply(z, q)
-
-    share_out(z)
+    def whole(other):
+        multiply(other, True)
+        multiply(other, False)
+        share_out(other)
+
+    whole(z)
 
     @pl.loop(1, chips)
     def _(d):
-        @pl.loop(0, parts)
-        def _(q):
+        for q in range(parts // 2):
             sides(d, functools.partial(arrive, q))
-            sides(d, lambda other, side: multiply(other, q))
-            pl.when(q == parts // 2 - 1)(lambda: sides(d - 1, lambda other, side: finish(other)))
-
-        sides(d, lambda other, side: share_out(other))
+        sides(d, lambda other, side: multiply(other, True))
+        sides(d - 1, lambda other, side: finish(other))
+        for q in range(parts // 2, parts):
+            sides(d, functools.partial(arrive, q))
+
+        def last(other, side):
+            multiply(other, False)
+            share_out(other)
+
+        sides(d, last)
 
     sides(chips - 1, lambda other, side: finish(other))
 
@@ -442,6 +442,7 @@
         scratch_shapes=[
             pltpu.VMEM(x.shape, bf16),
             pltpu.VMEM(taps.shape, f32),
+            pltpu.VMEM((modes, channels), f32),
             pltpu.VMEM((modes, channels), f32),
             pltpu.VMEM((modes, channels), f32),
             pltpu.VMEM((1, channels), f32),

time: 107 us -> 85.5 us (0.80)
  Pallas kernels: 105 us -> 83.4 us
    pallas_call x1, Pallas kernels: 105 us -> 83.4 us  [block(): pl.pallas_call(functools.partial(block_kernel, n_ctx, n_tp), out_shape=ja...]
where the time goes in v3:
time: 85.5 us; the launch traced here: 85.3 us
  Pallas kernels  83.4 us (98%)
  local copies, waits for them, and re-layouts  1.88 us (2%)
    pallas_call x1, Pallas kernels, block(): pl.pallas_call(functools.partial(block_kernel, n_ctx, n_tp), out_shape=ja...  83.4 us
    unnamed x1, local copies, waits for them, and re-layouts  1.88 us

profile of v3, /device:TPU:6, one launch (start us, length us, event | category | flops | bytes accessed | tf_op | source)
XLA Modules:
  0.0 85.3 jit_solution(3133252110047793366)
XLA Ops:
  0.0 83.4 %block.1 = bf16[128,2048]{1,0:T(8,128)(2,1)} custom-call(bf16[3,128,2048]{2,1,0:T(8,128)(2,1)} %bitcast.2, f32[3,3,2048]{2,1,0:T(4,128)} %taps_hbm.1, f32[16,2048]{1,0:T(8,128)} %rate_hbm.1, f32[16,2048]{1,0:T(8,128)} %residue_hbm.1, f32[1,2048]{1,0:T(1,128)} %bitcast.3, bf16[2048,1024]{1,0:T(8,128)(2,1)} %w_hbm.1), custom_call_target="tpu_custom_call" | custom-call | tf_op jit(solution)/shard_map/block/pallas_call | solution.py:437
  83.4 1.9 %copy.8 = bf16[128,2048]{1,0:T(8,128)(2,1)} copy(bf16[128,2048]{1,0:T(8,128)(2,1)} %block.1) | data formatting | bytes 1048576

commit v4 on v3

--- a/solution.py
+++ b/solution.py
@@ -319,7 +319,7 @@
     def sides(d, work):
         for side in range(2):
             other = z - d if side == 0 else z + d
-            valid = (other >= 0) if side == 0 else ((other < chips) & (d > 0))
+            valid = ((other >= 0) & (d >= 0)) if side == 0 else ((other < chips) & (d > 0))
             pl.when(valid)(functools.partial(work, other, side))
 
     def arrive(q, other, side):
@@ -352,29 +352,24 @@
 
     loads[5].wait()
 
-    def whole(other):
-        multiply(other, True)
-        multiply(other, False)
-        share_out(other)
-
-    whole(z)
-
-    @pl.loop(1, chips)
+    behind = jnp.where((z > 0) & (z < chips - 1), 1, 0)
+
+    @pl.loop(0, chips + 1)
     def _(d):
-        for q in range(parts // 2):
-            sides(d, functools.partial(arrive, q))
-        sides(d, lambda other, side: multiply(other, True))
-        sides(d - 1, lambda other, side: finish(other))
-        for q in range(parts // 2, parts):
-            sides(d, functools.partial(arrive, q))
-
-        def last(other, side):
-            multiply(other, False)
-            share_out(other)
-
-        sides(d, last)
-
-    sides(chips - 1, lambda other, side: finish(other))
+        ready = d - behind
+        for first in (True, False):
+            chunks = range(parts // 2) if first else range(parts // 2, parts)
+
+            def take(other, side):
+                for q in chunks:
+                    arrive(q, other, side)
+
+            pl.when(d > 0)(lambda: sides(d, take))
+            sides(ready, lambda other, side: multiply(other, first))
+        sides(ready, lambda other, side: share_out(other))
+        sides(ready - 1, lambda other, side: finish(other))
+
+    pl.when(behind == 1)(lambda: sides(chips - 1, lambda other, side: finish(other)))
 
     @pl.loop(0, per * half)
     def _(k):

time: 85.5 us -> 75.8 us (0.89)
  the two profiles are of different devices: /device:TPU:6 before, /device:TPU:4 now
where the time goes in v4:
time: 75.8 us; the launch traced here: 75.7 us
  Pallas kernels  73.8 us (97%)
  local copies, waits for them, and re-layouts  1.88 us (2%)
    pallas_call x1, Pallas kernels, block(): pl.pallas_call(functools.partial(block_kernel, n_ctx, n_tp), out_shape=ja...  73.8 us
    unnamed x1, local copies, waits for them, and re-layouts  1.88 us

profile of v4, /device:TPU:4, one launch (start us, length us, event | category | flops | bytes accessed | tf_op | source)
XLA Modules:
  0.0 75.7 jit_solution(1969605934058908125)
XLA Ops:
  0.0 73.8 %block.1 = bf16[128,2048]{1,0:T(8,128)(2,1)} custom-call(bf16[3,128,2048]{2,1,0:T(8,128)(2,1)} %bitcast.2, f32[3,3,2048]{2,1,0:T(4,128)} %taps_hbm.1, f32[16,2048]{1,0:T(8,128)} %rate_hbm.1, f32[16,2048]{1,0:T(8,128)} %residue_hbm.1, f32[1,2048]{1,0:T(1,128)} %bitcast.3, bf16[2048,1024]{1,0:T(8,128)(2,1)} %w_hbm.1), custom_call_target="tpu_custom_call" | custom-call | tf_op jit(solution)/shard_map/block/pallas_call | solution.py:432
  73.8 1.9 %copy.8 = bf16[128,2048]{1,0:T(8,128)(2,1)} copy(bf16[128,2048]{1,0:T(8,128)(2,1)} %block.1) | data formatting | bytes 1048576

commit v5 on v4

--- a/solution.py
+++ b/solution.py
@@ -12,7 +12,7 @@
 LANES = 128
 HALO = 8
 TAIL = 16
-PARTS = 4
+PARTS = 8
 
 
 def spread(row):
@@ -90,27 +90,28 @@
 
     expected = (n_ctx - 1) + (n_tp - 1) + chips + per * half
 
-    @pl.when(mine)
-    def _():
-        pl.semaphore_wait(barrier, expected - 2)
-
-    @pl.when(~mine)
-    def _():
-        pl.semaphore_wait(barrier, expected)
-
-    def remote(src, dst, send, recv, ctx, tp):
-        return pltpu.make_async_remote_copy(
-            src_ref=src, dst_ref=dst, send_sem=send, recv_sem=recv,
-            device_id=at(ctx, tp), device_id_type=MESH,
-        )
-
-    to_next = remote(halo_out, halo_in, halo_sem.at[0], halo_sem.at[1], c + 1, t)
     for copy in loads[:5]:
         copy.wait()
     for feature in range(3):
         tail = x_ref[feature, pl.ds(positions - TAIL, TAIL), :].astype(jnp.float32)
         halo_out[pl.ds(2 * feature, 2), :] = tail[TAIL - 2 :]
     halo_out[pl.ds(6, 2), :] = jnp.zeros((2, channels), jnp.float32)
+
+    @pl.when(mine)
+    def _():
+        pl.semaphore_wait(barrier, expected - 2)
+
+    @pl.when(~mine)
+    def _():
+        pl.semaphore_wait(barrier, expected)
+
+    def remote(src, dst, send, recv, ctx, tp):
+        return pltpu.make_async_remote_copy(
+            src_ref=src, dst_ref=dst, send_sem=send, recv_sem=recv,
+            device_id=at(ctx, tp), device_id_type=MESH,
+        )
+
+    to_next = remote(halo_out, halo_in, halo_sem.at[0], halo_sem.at[1], c + 1, t)
     pl.when(c < n_ctx - 1)(lambda: to_next.start())
 
     twice = -2.0 * rate_ref[...]
@@ -275,7 +276,15 @@
     def is_home(other):
         return (2 * other + lax.div(t, half) == c) & (lax.div(c, per) == t)
 
-    tile = min(256, columns)
+    tile = min(256, wide)
+
+    def share_out(other, h):
+        @pl.loop(1, n_tp)
+        def _(k):
+            to_tp = lax.rem(t + k, n_tp)
+            rows = pl.ds(pl.multiple_of(to_tp * share, share), share)
+            psend[other, to_tp, h] = part[other, rows, pl.ds(h * wide, wide)].astype(jnp.bfloat16)
+            p_copy(other, k, h).start()
 
     def multiply(other, first):
         chunks = range(parts // 2) if first else range(parts // 2, parts)
@@ -283,19 +292,13 @@
             from_sibling(other, q).wait_recv()
         rows = jnp.concatenate([gbuf[other, :, q].reshape(2 * positions, width) for q in chunks], axis=1)
         depth = pl.ds(chunks[0] * width, len(chunks) * width)
-        for j in range(columns // tile):
-            cols = pl.ds(j * tile, tile)
-            product = jnp.dot(rows, w_ref[depth, cols], preferred_element_type=jnp.float32)
-            part[other, :, cols] = product if first else part[other, :, cols] + product
-
-    def share_out(other):
         for h in range(2):
-            @pl.loop(1, n_tp)
-            def _(k):
-                to_tp = lax.rem(t + k, n_tp)
-                rows = pl.ds(pl.multiple_of(to_tp * share, share), share)
-                psend[other, to_tp, h] = part[other, rows, pl.ds(h * wide, wide)].astype(jnp.bfloat16)
-                p_copy(other, k, h).start()
+            for j in range(wide // tile):
+                cols = pl.ds(h * wide + j * tile, tile)
+                product = jnp.dot(rows, w_ref[depth, cols], preferred_element_type=jnp.float32)
+                part[other, :, cols] = product if first else part[other, :, cols] + product
+            if not first:
+                share_out(other, h)
 
     def finish(other):
         for h in range(2):
@@ -366,7 +369,6 @@
 
             pl.when(d > 0)(lambda: sides(d, take))
             sides(ready, lambda other, side: multiply(other, first))
-        sides(ready, lambda other, side: share_out(other))
         sides(ready - 1, lambda other, side: finish(other))
 
     pl.when(behind == 1)(lambda: sides(chips - 1, lambda other, side: finish(other)))

time: 75.8 us -> 76.3 us (level)
  no operation moved by 1% of the time
where the time goes in v5:
time: 76.3 us; the launch traced here: 76.1 us
  Pallas kernels  74.2 us (97%)
  local copies, waits for them, and re-layouts  1.88 us (2%)
    pallas_call x1, Pallas kernels, block(): pl.pallas_call(functools.partial(block_kernel, n_ctx, n_tp), out_shape=ja...  74.2 us
    unnamed x1, local copies, waits for them, and re-layouts  1.88 us

profile of v5, /device:TPU:4, one launch (start us, length us, event | category | flops | bytes accessed | tf_op | source)
XLA Modules:
  0.0 76.1 jit_solution(8933056846252351764)
XLA Ops:
  0.0 74.2 %block.1 = bf16[128,2048]{1,0:T(8,128)(2,1)} custom-call(bf16[3,128,2048]{2,1,0:T(8,128)(2,1)} %bitcast.2, f32[3,3,2048]{2,1,0:T(4,128)} %taps_hbm.1, f32[16,2048]{1,0:T(8,128)} %rate_hbm.1, f32[16,2048]{1,0:T(8,128)} %residue_hbm.1, f32[1,2048]{1,0:T(1,128)} %bitcast.3, bf16[2048,1024]{1,0:T(8,128)(2,1)} %w_hbm.1), custom_call_target="tpu_custom_call" | custom-call | tf_op jit(solution)/shard_map/block/pallas_call | solution.py:434
  74.2 1.9 %copy.8 = bf16[128,2048]{1,0:T(8,128)(2,1)} copy(bf16[128,2048]{1,0:T(8,128)(2,1)} %block.1) | data formatting | bytes 1048576

commit v6 on v5

--- a/solution.py
+++ b/solution.py
@@ -12,7 +12,7 @@
 LANES = 128
 HALO = 8
 TAIL = 16
-PARTS = 8
+PARTS = 4
 
 
 def spread(row):
@@ -23,9 +23,9 @@
     n_ctx, n_tp, x_hbm, taps_hbm, rate_hbm, residue_hbm, skip_hbm, w_hbm, out_ref,
     x_ref, taps_ref, rate_ref, decay_ref, gain_ref, skip_ref, w_ref, load_sem,
     halo_out, halo_in, halo_sem, ext, rows_ref, q_ref, resp_ref, before_ref,
-    end_ref, sib_end, chip_end, chip_in, ends, carry, gbuf, part, pown, psend, prcv, fin, obuf,
+    end_ref, sib_end, chip_end, chip_in, ends, carry, gbuf, part, pown, psend, prcv, fin, rbuf, obuf,
     e_send, e_recv, c_send, c_recv, i_send, i_recv, up_sem, dn_sem, g_recv, sib_send, sib_recv,
-    p_send, p_recv, f_send, f_recv,
+    p_send, p_recv, f_send, f_recv, r_recv, s_send,
 ):
     chips = n_ctx // 2
     parts = end_ref.shape[0]
@@ -44,7 +44,7 @@
     t = lax.axis_index("tp")
     z, core = lax.div(c, 2), lax.rem(c, 2)
     sibling = c + 1 - 2 * core
-    mine = (lax.div(c, per) == t) & (core == lax.div(t, half))
+    passing = lax.div(t, half) == core
 
     def load(k, src, dst):
         return pltpu.make_async_copy(src, dst, load_sem.at[k])
@@ -72,24 +72,6 @@
     def _(k):
         greet(c, lax.rem(t + k, n_tp))
 
-    @pl.loop(0, chips)
-    def _(other):
-        to_ctx, to_tp = 2 * other + lax.div(t, half), lax.div(c, per)
-
-        @pl.when(~((to_ctx == c) & (to_tp == t)))
-        def _():
-            greet(to_ctx, to_tp)
-
-    @pl.loop(0, per * half)
-    def _(k):
-        from_ctx, from_tp = per * t + lax.div(k, half), core * half + lax.rem(k, half)
-
-        @pl.when(~((from_ctx == c) & (from_tp == t)))
-        def _():
-            greet(from_ctx, from_tp)
-
-    expected = (n_ctx - 1) + (n_tp - 1) + chips + per * half
-
     for copy in loads[:5]:
         copy.wait()
     for feature in range(3):
@@ -97,13 +79,7 @@
         halo_out[pl.ds(2 * feature, 2), :] = tail[TAIL - 2 :]
     halo_out[pl.ds(6, 2), :] = jnp.zeros((2, channels), jnp.float32)
 
-    @pl.when(mine)
-    def _():
-        pl.semaphore_wait(barrier, expected - 2)
-
-    @pl.when(~mine)
-    def _():
-        pl.semaphore_wait(barrier, expected)
+    pl.semaphore_wait(barrier, (n_ctx - 1) + (n_tp - 1))
 
     def remote(src, dst, send, recv, ctx, tp):
         return pltpu.make_async_remote_copy(
@@ -265,16 +241,27 @@
         )
 
     row0 = pl.multiple_of(lax.rem(t, half) * share, share)
-    col0 = pl.multiple_of(lax.rem(c, per) * columns, columns)
-
-    def home(other, h):
+
+    def along(other, h):
         return remote(
-            fin.at[other, h], obuf.at[pl.ds(row0, share), pl.ds(col0 + h * wide, wide)], f_send.at[other, h],
-            f_recv.at[lax.rem(c, per) * half + lax.rem(t, half), h], 2 * other + lax.div(t, half), lax.div(c, per),
+            fin.at[other, h], rbuf.at[c, h], f_send.at[other, h], r_recv.at[c, h], 2 * other + lax.div(t, half), t
         )
 
-    def is_home(other):
-        return (2 * other + lax.div(t, half) == c) & (lax.div(c, per) == t)
+    def from_along(source, h):
+        return remote(fin.at[0, h], rbuf.at[source, h], f_send.at[0, h], r_recv.at[source, h], source, t)
+
+    def stays(other):
+        return 2 * other + lax.div(t, half) == c
+
+    def place_of(source, h):
+        cols = pl.multiple_of(lax.rem(source, per) * columns, columns) + h * wide
+        return obuf.at[pl.ds(row0, share), pl.ds(pl.multiple_of(cols, wide), wide)]
+
+    def across(source, h, block):
+        return remote(
+            block, place_of(source, h), s_send.at[source, h],
+            f_recv.at[lax.rem(source, per) * half + lax.rem(t, half), h], c, lax.div(source, per),
+        )
 
     tile = min(256, wide)
 
@@ -311,13 +298,29 @@
 
             fin[other, h] = pown[...].astype(jnp.bfloat16)
 
-            @pl.when(is_home(other))
-            def _():
-                obuf[pl.ds(row0, share), pl.ds(col0 + h * wide, wide)] = fin[other, h]
-
-            @pl.when(~is_home(other))
-            def _():
-                home(other, h).start()
+            pl.when(~stays(other))(lambda: along(other, h).start())
+
+    def pass_one(source, h, block):
+        @pl.when(lax.div(source, per) == t)
+        def _():
+            place_of(source, h)[...] = block[...]
+
+        pl.when(lax.div(source, per) != t)(lambda: across(source, h, block).start())
+
+    def pass_on(other):
+        @pl.when(passing)
+        def _():
+            for k in range(2):
+                source = 2 * other + k
+                for h in range(2):
+                    @pl.when(source == c)
+                    def _():
+                        pass_one(source, h, fin.at[z, h])
+
+                    @pl.when(source != c)
+                    def _():
+                        from_along(source, h).wait_recv()
+                        pass_one(source, h, rbuf.at[source, h])
 
     def sides(d, work):
         for side in range(2):
@@ -370,20 +373,26 @@
             pl.when(d > 0)(lambda: sides(d, take))
             sides(ready, lambda other, side: multiply(other, first))
         sides(ready - 1, lambda other, side: finish(other))
-
-    pl.when(behind == 1)(lambda: sides(chips - 1, lambda other, side: finish(other)))
+        sides(ready - 2, lambda other, side: pass_on(other))
+
+    @pl.when(behind == 1)
+    def _():
+        sides(chips - 1, lambda other, side: finish(other))
+        sides(chips - 2, lambda other, side: pass_on(other))
+
+    sides(chips - 1, lambda other, side: pass_on(other))
 
     @pl.loop(0, per * half)
     def _(k):
-        from_ctx, from_tp = per * t + lax.div(k, half), core * half + lax.rem(k, half)
-
-        @pl.when(~((from_ctx == c) & (from_tp == t)))
+        from_tp = core * half + lax.rem(k, half)
+
+        @pl.when(from_tp != t)
         def _():
             rows = pl.multiple_of(lax.rem(k, half) * share, share)
             cols = pl.multiple_of(lax.div(k, half) * columns, columns)
             for h in range(2):
                 block = obuf.at[pl.ds(rows, share), pl.ds(cols + h * wide, wide)]
-                remote(fin.at[0, h], block, f_send.at[0, h], f_recv.at[k, h], from_ctx, from_tp).wait_recv()
+                remote(fin.at[0, h], block, s_send.at[0, h], f_recv.at[k, h], c, from_tp).wait_recv()
 
     out_ref[...] = obuf[...]
 
@@ -414,10 +423,17 @@
             for h in range(2):
                 p_copy(other, k, h).wait_send()
 
-        @pl.when(~is_home(other))
+        @pl.when(~stays(other))
         def _():
             for h in range(2):
-                home(other, h).wait_send()
+                along(other, h).wait_send()
+
+    @pl.loop(0, n_ctx)
+    def _(source):
+        @pl.when(passing & (lax.div(source, per) != t))
+        def _():
+            for h in range(2):
+                across(source, h, rbuf.at[source, h]).wait_send()
 
 
 def block(n_ctx, n_tp, x, taps, rate, residue, skip, w):
@@ -465,6 +481,7 @@
             pltpu.VMEM((chips, n_tp, 2, share, columns // 2), bf16),
             pltpu.VMEM((chips, n_tp - 1, 2, share, columns // 2), bf16),
             pltpu.VMEM((chips, 2, share, columns // 2), bf16),
+            pltpu.VMEM((n_ctx, 2, share, columns // 2), bf16),
             pltpu.VMEM((positions, out_cols), bf16),
             dma((parts,)),
             dma((parts,)),
@@ -481,6 +498,8 @@
             dma((chips, n_tp - 1, 2)),
             dma((chips, 2)),
             dma((n_ctx // n_tp * (n_tp // 2), 2)),
+            dma((n_ctx, 2)),
+            dma((n_ctx, 2)),
         ],
         compiler_params=pltpu.CompilerParams(
             collective_id=0, has_side_effects=True, vmem_limit_bytes=60 * 1024 * 1024

time: 76.3 us -> 75.8 us (level)
  the two profiles are of different devices: /device:TPU:4 before, /device:TPU:6 now
where the time goes in v6:
time: 75.8 us; the launch traced here: 75.7 us
  Pallas kernels  73.8 us (97%)
  local copies, waits for them, and re-layouts  1.88 us (2%)
    pallas_call x1, Pallas kernels, block(): pl.pallas_call(functools.partial(block_kernel, n_ctx, n_tp), out_shape=ja...  73.8 us
    unnamed x1, local copies, waits for them, and re-layouts  1.88 us

profile of v6, /device:TPU:6, one launch (start us, length us, event | category | flops | bytes accessed | tf_op | source)
XLA Modules:
  0.0 75.7 jit_solution(7809495308170166857)
XLA Ops:
  0.0 73.8 %block.1 = bf16[128,2048]{1,0:T(8,128)(2,1)} custom-call(bf16[3,128,2048]{2,1,0:T(8,128)(2,1)} %bitcast.2, f32[3,3,2048]{2,1,0:T(4,128)} %taps_hbm.1, f32[16,2048]{1,0:T(8,128)} %rate_hbm.1, f32[16,2048]{1,0:T(8,128)} %residue_hbm.1, f32[1,2048]{1,0:T(1,128)} %bitcast.3, bf16[2048,1024]{1,0:T(8,128)(2,1)} %w_hbm.1), custom_call_target="tpu_custom_call" | custom-call | tf_op jit(solution)/shard_map/block/pallas_call | solution.py:450
  73.8 1.9 %copy.8 = bf16[128,2048]{1,0:T(8,128)(2,1)} copy(bf16[128,2048]{1,0:T(8,128)(2,1)} %block.1) | data formatting | bytes 1048576

commit v7 on v6

--- a/solution.py
+++ b/solution.py
@@ -12,7 +12,7 @@
 LANES = 128
 HALO = 8
 TAIL = 16
-PARTS = 4
+PARTS = 2
 
 
 def spread(row):

time: 75.8 us -> 78.2 us (1.032)
  Pallas kernels: 73.8 us -> 76.1 us
    pallas_call x1, Pallas kernels: 73.8 us -> 76.1 us  [block(): pl.pallas_call(functools.partial(block_kernel, n_ctx, n_tp), out_shape=ja...]
where the time goes in v7:
time: 78.2 us; the launch traced here: 78 us
  Pallas kernels  76.1 us (97%)
  local copies, waits for them, and re-layouts  1.88 us (2%)
    pallas_call x1, Pallas kernels, block(): pl.pallas_call(functools.partial(block_kernel, n_ctx, n_tp), out_shape=ja...  76.1 us
    unnamed x1, local copies, waits for them, and re-layouts  1.88 us

profile of v7, /device:TPU:6, one launch (start us, length us, event | category | flops | bytes accessed | tf_op | source)
XLA Modules:
  0.0 78.0 jit_solution(15264924128313026795)
XLA Ops:
  0.0 76.1 %block.1 = bf16[128,2048]{1,0:T(8,128)(2,1)} custom-call(bf16[3,128,2048]{2,1,0:T(8,128)(2,1)} %bitcast.2, f32[3,3,2048]{2,1,0:T(4,128)} %taps_hbm.1, f32[16,2048]{1,0:T(8,128)} %rate_hbm.1, f32[16,2048]{1,0:T(8,128)} %residue_hbm.1, f32[1,2048]{1,0:T(1,128)} %bitcast.3, bf16[2048,1024]{1,0:T(8,128)(2,1)} %w_hbm.1), custom_call_target="tpu_custom_call" | custom-call | tf_op jit(solution)/shard_map/block/pallas_call | solution.py:450
  76.1 1.9 %copy.8 = bf16[128,2048]{1,0:T(8,128)(2,1)} copy(bf16[128,2048]{1,0:T(8,128)(2,1)} %block.1) | data formatting | bytes 1048576
